TPU v7x, 32 devices: a whole 2x2x4 slice. The times are simulated.
32 devices in a mesh: tm: 4 (over y, x), feed: 8 (over z, core).
Axes of the slice: x: 2, y: 2, z: 4, core: 2. Of those that a mesh axis runs over, the one named last changes fastest.
Arguments:
- voltages: bfloat16 [2048, 98304], P('feed', 'tm'), may hold values from -6 to 6
- gains: bfloat16 [2, 2048, 1024], P(None, 'feed'), may hold values from -4 to 4
- beam_weights: bfloat16 [2, 2048, 2048], replicated, may hold values from -0.09375 to 0.09375
- delay_filter: float32 [1024, 1024], replicated, may hold values from -0.21875 to 0.21875
- channel_lists: int32 [8, 192], replicated, may hold values from -1 to 1023, as said below
- beam_order: int32 [2048], replicated, may hold values from 0 to 2047, each once
Outputs:
- filtered: float32 [4, 2048, 1024], P('tm', 'feed')
Inputs may be any that keep to these rules, and one draw needn't show every extreme that they name: `channel_lists`: each row holds distinct channel numbers in its first places and -1 in the rest; 768 channel numbers are listed in all, none twice; a row lists 0 to 192 channels, and some row lists exactly 192.
All inputs are finite; a program needn't handle non-finite values.
Results may differ from a plain program's by a relative error of at most 0.0021.
Values may be sent and summed in bfloat16 or wider, within the bound.
A program may use at most 192 MiB of HBM per device.

v0:
```python
import functools

import jax
import jax.numpy as jnp
import numpy as np
from jax import lax
from jax.experimental import pallas as pl
from jax.experimental.pallas import tpu as pltpu
from jax.sharding import PartitionSpec as P

FFT = 2048
CHANNELS = 1024
LIVE = 768
VMEM = 56 * 1024 * 1024
BF = jnp.bfloat16
F32 = jnp.float32
PARTS = ((3, 3), (6, 6), (0, 3))
NT = (((1,), (1,)), ((), ()))


def from_behind(block, axis, distance):
    devices = range(lax.axis_size(axis))
    route = [(i - distance, i) for i in devices if i - distance in devices]
    return lax.ppermute(block, axis, route)


def make_window(length):
    places = jnp.arange(4 * length, dtype=F32)
    centred = (places - 2.0 * length + 0.5) / length
    taper = 0.5 - 0.5 * jnp.cos(2.0 * jnp.pi * (places + 0.5) / (4.0 * length))
    return (jnp.sinc(centred) * taper).reshape(4, length)


def make_table(length):
    channel_rows = np.arange(length // 2, dtype=np.int32)[:, None]
    sample_cols = np.arange(length, dtype=np.int32)[None, :]
    phases = (channel_rows * sample_cols % length).astype(np.float32)
    angles = np.float32(2.0 * np.pi) * phases / np.float32(length)
    scaling = np.float32(length ** (-0.5))
    return np.stack([np.cos(angles) * scaling, -np.sin(angles) * scaling]).astype(BF)


def bank_kernel(groups, hist_ref, frame_ref, window_ref, table_ref, gain_ref, out_ref, past):
    step = pl.program_id(0)

    @pl.when(step == 0)
    def _():
        for t in range(3):
            past[t] = hist_ref[:, t * FFT : (t + 1) * FFT]

    now = frame_ref[...]
    total = window_ref[0:1, :] * past[lax.rem(step, 3)].astype(F32)
    total = total + window_ref[1:2, :] * past[lax.rem(step + 1, 3)].astype(F32)
    total = total + window_ref[2:3, :] * past[lax.rem(step + 2, 3)].astype(F32)
    total = total + window_ref[3:4, :] * now.astype(F32)
    past[lax.rem(step, 3)] = now
    weighted = total.astype(BF)
    table = table_ref[...].reshape(2 * LIVE, FFT)
    spectra = lax.dot_general(table, weighted, NT, preferred_element_type=F32)
    real, imag = spectra[:LIVE], spectra[LIVE:]
    gr = gain_ref[0].astype(F32)
    gi = gain_ref[1].astype(F32)
    gained_real = (real * gr - imag * gi).astype(BF)
    gained_imag = (real * gi + imag * gr).astype(BF)
    slots = LIVE // groups
    for g in range(groups):
        out_ref[g, 0, 0] = gained_real[g * slots : (g + 1) * slots]
        out_ref[g, 1, 0] = gained_imag[g * slots : (g + 1) * slots]


def bank(earlier, voltages, window, table, gain, groups, first, count):
    inputs = voltages.shape[0]
    slots = LIVE // groups
    hist = earlier if first == 0 else voltages
    place = 0 if first == 0 else first // 3 - 1
    return pl.pallas_call(
        functools.partial(bank_kernel, groups),
        grid=(count,),
        out_shape=jax.ShapeDtypeStruct((groups, 2, count, slots, inputs), BF),
        in_specs=[
            pl.BlockSpec((inputs, 3 * FFT), lambda k: (0, place)),
            pl.BlockSpec((inputs, FFT), lambda k: (0, first + k)),
            pl.BlockSpec((4, FFT), lambda k: (0, 0)),
            pl.BlockSpec((2, LIVE, FFT), lambda k: (0, 0, 0)),
            pl.BlockSpec((2, LIVE, inputs), lambda k: (0, 0, 0)),
        ],
        out_specs=pl.BlockSpec((groups, 2, 1, slots, inputs), lambda k: (0, 0, k, 0, 0)),
        scratch_shapes=[pltpu.VMEM((3, inputs, FFT), BF)],
        compiler_params=pltpu.CompilerParams(vmem_limit_bytes=VMEM),
        cost_estimate=pl.CostEstimate(
            flops=4 * count * inputs * FFT * LIVE,
            bytes_accessed=2 * count * inputs * (FFT + 2 * LIVE) + 4 * LIVE * FFT,
            transcendentals=0,
        ),
    )(hist, voltages, window, table, gain)


def beam_kernel(got_ref, weight_ref, before_ref, out_ref, held):
    groups, _, count, slots, inputs = got_ref.shape
    rows = count * slots

    @pl.when(pl.program_id(0) == 0)
    def _():
        for g in range(groups):
            cols = slice(g * inputs, (g + 1) * inputs)
            held[:, cols] = got_ref[g].reshape(2 * rows, inputs)

    by_real = lax.dot_general(held[...], weight_ref[0], NT, preferred_element_type=F32)
    by_imag = lax.dot_general(held[...], weight_ref[1], NT, preferred_element_type=F32)
    real = by_real[:rows] - by_imag[rows:]
    imag = by_real[rows:] + by_imag[:rows]
    power = (real * real + imag * imag).reshape(count, slots, real.shape[1])
    out_ref[...] = before_ref[...] + jnp.sum(power, axis=0)


def beams(got, weights, before):
    groups, _, count, slots, inputs = got.shape
    total, deep = weights.shape[1:]
    tile = 256
    return pl.pallas_call(
        beam_kernel,
        grid=(total // tile,),
        out_shape=jax.ShapeDtypeStruct((slots, total), F32),
        in_specs=[
            pl.BlockSpec(got.shape, lambda b: (0, 0, 0, 0, 0)),
            pl.BlockSpec((2, tile, deep), lambda b: (0, b, 0)),
            pl.BlockSpec((slots, tile), lambda b: (0, b)),
        ],
        out_specs=pl.BlockSpec((slots, tile), lambda b: (0, b)),
        scratch_shapes=[pltpu.VMEM((2 * count * slots, deep), BF)],
        compiler_params=pltpu.CompilerParams(vmem_limit_bytes=VMEM),
        cost_estimate=pl.CostEstimate(
            flops=8 * count * slots * deep * total,
            bytes_accessed=4 * total * deep + 4 * count * slots * deep,
            transcendentals=0,
        ),
    )(got, weights, before)


def plain_bank(earlier, voltages, window, table, gain, groups, first, count):
    inputs = voltages.shape[0]
    whole = jnp.concatenate([earlier, voltages], axis=1).reshape(inputs, -1, FFT)
    total = 0.0
    for t in range(4):
        total = total + window[t] * whole[:, first + t : first + t + count].astype(F32)
    spectra = jnp.einsum("rcn,ikn->rkci", table, total.astype(BF), preferred_element_type=F32)
    gr, gi = gain[0].astype(F32), gain[1].astype(F32)
    real, imag = spectra[0], spectra[1]
    gained = jnp.stack([real * gr - imag * gi, real * gi + imag * gr]).astype(BF)
    gained = gained.reshape(2, count, groups, LIVE // groups, inputs)
    return jnp.transpose(gained, (2, 0, 1, 3, 4))


def plain_beams(got, weights, before):
    groups, _, count, slots, inputs = got.shape
    flat = jnp.transpose(got, (1, 2, 3, 0, 4)).reshape(2, count * slots, groups * inputs)
    parts = jnp.einsum("xri,ybi->xyrb", flat, weights, preferred_element_type=F32)
    real, imag = parts[0, 0] - parts[1, 1], parts[0, 1] + parts[1, 0]
    power = (real * real + imag * imag).reshape(count, slots, -1)
    return before + jnp.sum(power, axis=0)


def body(voltages, gains, beam_weights, delay_filter, channel_lists, beam_order):
    groups = lax.axis_size("feed")
    inputs = voltages.shape[0]
    frames_here = voltages.shape[1] // FFT
    total_beams = beam_weights.shape[1]
    slots = LIVE // groups
    aligned = inputs % 128 == 0 and slots % 16 == 0
    run_bank, run_beams = (bank, beams) if aligned else (plain_bank, plain_beams)
    earlier = from_behind(voltages[:, (frames_here - 3) * FFT :], "tm", 1)
    window = make_window(FFT)

    numbers = jnp.arange(CHANNELS, dtype=jnp.int32)
    live = jnp.any(channel_lists.reshape(-1)[:, None] == numbers[None, :], axis=0)
    below = (numbers[:, None] < numbers[None, :]).astype(BF)
    rank = jnp.dot(live.astype(BF)[None, :], below, preferred_element_type=F32)[0]
    rank = rank.astype(jnp.int32)
    places = jnp.arange(LIVE, dtype=jnp.int32)[:, None]
    pick = ((rank[None, :] == places) & live[None, :]).astype(BF)

    table = jnp.einsum("sc,rcn->rsn", pick, jnp.asarray(make_table(FFT)))
    gain = jnp.einsum("sc,ric->rsi", pick, gains)
    rows = jnp.dot(pick.astype(F32), delay_filter, precision=lax.Precision.HIGHEST)
    order = (beam_order[None, :] == jnp.arange(total_beams, dtype=jnp.int32)[:, None]).astype(BF)

    powers = jnp.zeros((slots, total_beams), F32)
    outgoing = [
        run_bank(earlier, voltages, window, table, gain, groups, first, count)
        for first, count in PARTS
    ]
    for at, block in enumerate(outgoing):
        got = lax.all_to_all(block, "feed", split_axis=0, concat_axis=0, tiled=True)
        if at == len(outgoing) - 1:
            powers, rows = lax.optimization_barrier((powers, rows))
        powers = run_beams(got, beam_weights, powers)
    powers = powers * (1.0 / frames_here)
    high = powers.astype(BF)
    low = (powers - high.astype(F32)).astype(BF)
    ordered = jnp.dot(jnp.concatenate([high, low], axis=0), order, preferred_element_type=F32)
    ordered = ordered[:slots] + ordered[slots:]
    ordered = jnp.transpose(ordered.reshape(slots, groups, total_beams // groups), (1, 0, 2))
    owned = lax.all_to_all(ordered, "feed", split_axis=0, concat_axis=0, tiled=True)
    owned = owned.reshape(LIVE, total_beams // groups)
    filtered = lax.dot_general(
        owned, rows, (((0,), (0,)), ((), ())), precision=lax.Precision.HIGHEST,
        preferred_element_type=F32,
    )
    return filtered[None]


def solution(mesh):
    placed = (P("feed", "tm"), P(None, "feed", None), P(), P(), P(), P())
    return jax.shard_map(
        body, mesh=mesh, in_specs=placed, out_specs=P("tm", "feed", None), check_vma=False
    )
```

profile of v0, /device:TPU:0, one launch (start us, length us, event | category | flops | bytes accessed | tf_op | source)
XLA Modules:
  0.0 309.3 jit_solution(6393887586029762039)
XLA Ops:
  0.0 0.0 copy-start
  0.0 0.9 fusion.28.window_ref
  0.9 0.8 eq.76
  1.7 0.9 fusion.2
  2.6 0.3 fusion.3
  2.9 11.9 %convolution_bitcast_fusion.table_ref = bf16[2,768,2048]{2,1,0:T(8,128)(2,1)} fusion(bf16[2,1024,2048]{2,1,0:T(8,128)(2,1)} %constant.62.clone, s32[1024]{0:T(1024)S(1)} %convert_element_type.24, pred[1024]{0:T(1024)(128)(4,1)S(1)} %fusion.2), kind=kOutput, calls=%fused_computation.7 | convolution fusion | flops 6444023808 | bytes 14685184 | tf_op jit(solution)/shard_map/sc,rcn->rsn/dot_general | solution.py:182
  14.8 0.0 copy-done
  14.8 1.9 fusion.17.gain_ref
  16.7 12.5 %shard_map.75 = bf16[8,2,3,96,256]{4,3,2,1,0:T(8,128)(2,1)} custom-call(bf16[256,24576]{1,0:T(8,128)(2,1)} %frame_ref.5, bf16[256,24576]{1,0:T(8,128)(2,1)} %frame_ref.5, f32[4,2048]{1,0:T(4,128)} %fusion.28.window_ref, bf16[2,768,2048]{2,1,0:T(8,128)(2,1)} %convolution_bitcast_fusion.table_ref, bf16[2,768,256]{2,1,0:T(8,128)(2,1)} %fusion.17.gain_ref), custom_call_target="tpu_custom_call" | custom-call | flops 4831838208 | bytes 11796480 | tf_op jit(solution)/shard_map/pallas_call | solution.py:76
  29.3 6.3 %all-to-all-start.2 = ((bf16[8,2,3,96,256]{4,3,2,1,0:T(8,128)(2,1)}), bf16[8,2,3,96,256]{4,3,2,1,0:T(8,128)(2,1)S(1)}, u32[]{:S(2)}, u32[]{:S(2)}) async-start(bf16[8,2,3,96,256]{4,3,2,1,0:T(8,128)(2,1)} %shard_map.75), calls=%async_computation.2 | async-start | bytes 4718592 | tf_op jit(solution)/shard_map/all_to_all | solution.py:193
  35.6 20.1 %shard_map.74 = bf16[8,2,6,96,256]{4,3,2,1,0:T(8,128)(2,1)} custom-call(bf16[256,24576]{1,0:T(8,128)(2,1)} %frame_ref.5, bf16[256,24576]{1,0:T(8,128)(2,1)} %frame_ref.5, f32[4,2048]{1,0:T(4,128)} %fusion.28.window_ref, bf16[2,768,2048]{2,1,0:T(8,128)(2,1)} %convolution_bitcast_fusion.table_ref, bf16[2,768,256]{2,1,0:T(8,128)(2,1)} %fusion.17.gain_ref), custom_call_target="tpu_custom_call" | custom-call | flops 9663676416 | bytes 17301504 | tf_op jit(solution)/shard_map/pallas_call | solution.py:76
  55.7 34.6 %all-to-all-done.2.got_ref = bf16[8,2,3,96,256]{4,3,2,1,0:T(8,128)(2,1)S(1)} async-done(((bf16[8,2,3,96,256]{4,3,2,1,0:T(8,128)(2,1)}), bf16[8,2,3,96,256]{4,3,2,1,0:T(8,128)(2,1)S(1)}, u32[]{:S(2)}, u32[]{:S(2)}) %all-to-all-start.2) | async-done | bytes 2359328 | tf_op jit(solution)/shard_map/all_to_all | solution.py:193
  90.3 0.0 copy-start.4
  90.3 1.5 copy-done.4
  91.7 4.6 %all-to-all-start.1 = ((bf16[8,2,6,96,256]{4,3,2,1,0:T(8,128)(2,1)}), bf16[8,2,6,96,256]{4,3,2,1,0:T(8,128)(2,1)}, u32[]{:S(2)}, u32[]{:S(2)}) async-start(bf16[8,2,6,96,256]{4,3,2,1,0:T(8,128)(2,1)} %shard_map.74), calls=%async_computation.1 | async-start | bytes 9437184 | tf_op jit(solution)/shard_map/all_to_all | solution.py:193
  96.4 2.2 slice.9
  98.6 3.8 %collective-permute-start = (bf16[256,6144]{1,0:T(8,128)(2,1)S(1)}, bf16[256,6144]{1,0:T(8,128)(2,1)S(1)}, u32[]{:S(2)}, u32[]{:S(2)}) collective-permute-start(bf16[256,6144]{1,0:T(8,128)(2,1)S(1)} %slice.9), channel_id=1, source_target_pairs={{0,8},{8,16},{16,24},{1,9},{9,17},{17,25},{2,10},{10,18},{18,26},{... | collective-permute-start | bytes 9437192 | tf_op jit(solution)/shard_map/ppermute | solution.py:24
  102.4 67.5 %collective-permute-done.hist_ref = bf16[256,6144]{1,0:T(8,128)(2,1)S(1)} collective-permute-done((bf16[256,6144]{1,0:T(8,128)(2,1)S(1)}, bf16[256,6144]{1,0:T(8,128)(2,1)S(1)}, u32[]{:S(2)}, u32[]{:S(2)}) %collective-permute-start) | collective-permute-done | bytes 3145760 | tf_op jit(solution)/shard_map/ppermute | solution.py:24
  169.9 0.0 copy-start.2
  169.9 1.6 copy-done.2
  171.5 12.6 %shard_map.73 = bf16[8,2,3,96,256]{4,3,2,1,0:T(8,128)(2,1)} custom-call(bf16[256,6144]{1,0:T(8,128)(2,1)} %copy-done.2, bf16[256,24576]{1,0:T(8,128)(2,1)} %frame_ref.5, f32[4,2048]{1,0:T(4,128)} %fusion.28.window_ref, bf16[2,768,2048]{2,1,0:T(8,128)(2,1)} %convolution_bitcast_fusion.table_ref, bf16[2,768,256]{2,1,0:T(8,128)(2,1)} %fusion.17.gain_ref), custom_call_target="tpu_custom_call" | custom-call | flops 4831838208 | bytes 11796480 | tf_op jit(solution)/shard_map/pallas_call | solution.py:76
  184.1 17.5 %all-to-all-done.1.got_ref = bf16[8,2,6,96,256]{4,3,2,1,0:T(8,128)(2,1)} async-done(((bf16[8,2,6,96,256]{4,3,2,1,0:T(8,128)(2,1)}), bf16[8,2,6,96,256]{4,3,2,1,0:T(8,128)(2,1)}, u32[]{:S(2)}, u32[]{:S(2)}) %all-to-all-start.1) | async-done | bytes 4718624 | tf_op jit(solution)/shard_map/all_to_all | solution.py:193
  201.6 3.6 %all-to-all-start = ((bf16[8,2,3,96,256]{4,3,2,1,0:T(8,128)(2,1)}), bf16[8,2,3,96,256]{4,3,2,1,0:T(8,128)(2,1)S(1)}, u32[]{:S(2)}, u32[]{:S(2)}) async-start(bf16[8,2,3,96,256]{4,3,2,1,0:T(8,128)(2,1)} %shard_map.73), calls=%async_computation | async-start | bytes 4718592 | tf_op jit(solution)/shard_map/all_to_all | solution.py:193
  205.2 8.4 %fusion.5 = f32[768,1024]{1,0:T(8,128)} fusion(f32[1024,1024]{1,0:T(8,128)} %param.10, s32[1024]{0:T(1024)S(1)} %convert_element_type.24, pred[1024]{0:T(1024)(128)(4,1)S(1)} %fusion.2), kind=kOutput, calls=%fused_computation.10 | convolution fusion | flops 9665249280 | bytes 7345152 | tf_op jit(solution)/shard_map/dot_general | solution.py:184
  213.7 1.0 broadcast_in_dim.9.before_ref
  214.6 15.5 %shard_map.76.before_ref = f32[96,2048]{1,0:T(8,128)} custom-call(bf16[8,2,3,96,256]{4,3,2,1,0:T(8,128)(2,1)} %copy-done.4, bf16[2,2048,2048]{2,1,0:T(8,128)(2,1)} %weight_ref.5, f32[96,2048]{1,0:T(8,128)} %broadcast_in_dim.9.before_ref), custom_call_target="tpu_custom_call" | custom-call | flops 9663676416 | bytes 19136512 | tf_op jit(solution)/shard_map/pallas_call | solution.py:120
  230.1 25.9 %shard_map.77.before_ref = f32[96,2048]{1,0:T(8,128)} custom-call(bf16[8,2,6,96,256]{4,3,2,1,0:T(8,128)(2,1)} %all-to-all-done.1.got_ref, bf16[2,2048,2048]{2,1,0:T(8,128)(2,1)} %weight_ref.5, f32[96,2048]{1,0:T(8,128)} %shard_map.76.before_ref), custom_call_target="tpu_custom_call" | custom-call | flops 19327352832 | bytes 21495808 | tf_op jit(solution)/shard_map/pallas_call | solution.py:120
  256.1 0.0 copy-start.6
  256.1 3.7 %all-to-all-done.got_ref = bf16[8,2,3,96,256]{4,3,2,1,0:T(8,128)(2,1)S(1)} async-done(((bf16[8,2,3,96,256]{4,3,2,1,0:T(8,128)(2,1)}), bf16[8,2,3,96,256]{4,3,2,1,0:T(8,128)(2,1)S(1)}, u32[]{:S(2)}, u32[]{:S(2)}) %all-to-all-start) | async-done | bytes 2359328 | tf_op jit(solution)/shard_map/all_to_all | solution.py:193
  259.8 0.0 copy-start.5
  259.8 1.5 copy-done.5
  261.3 15.5 %shard_map.78 = f32[96,2048]{1,0:T(8,128)} custom-call(bf16[8,2,3,96,256]{4,3,2,1,0:T(8,128)(2,1)} %copy-done.5, bf16[2,2048,2048]{2,1,0:T(8,128)(2,1)} %weight_ref.5, f32[96,2048]{1,0:T(8,128)} %shard_map.77.before_ref), custom_call_target="tpu_custom_call" | custom-call | flops 9663676416 | bytes 19136512 | tf_op jit(solution)/shard_map/pallas_call | solution.py:120
  276.8 1.2 multiply_convert_fusion
  278.1 0.0 copy-done.6
  278.1 3.7 %fusion = f32[192,2048]{1,0:T(8,128)S(1)} fusion(s32[2048]{0:T(1024)S(1)} %copy-done.6, bf16[96,2048]{1,0:T(8,128)(2,1)S(1)} %get-tuple-element.10, bf16[96,2048]{1,0:T(8,128)(2,1)S(1)} %get-tuple-element.9), kind=kOutput, calls=%fused_computation.1 | convolution fusion | flops 1616379904 | bytes 2367488 | tf_op jit(solution)/shard_map/dot_general | solution.py:200
  281.8 0.0 copy-start.3
  281.8 0.1 slice_add_fusion
  281.9 0.1 copy.12
  281.9 0.0 copy-start.1
  281.9 23.7 %all_to_all.20 = f32[8,96,256]{2,1,0:T(8,128)S(1)} all-to-all(f32[8,96,256]{2,1,0:T(8,128)S(1)} %bitcast.28), channel_id=1, replica_groups=mesh['tm'=4,'feed'=8] {'feed'}, dimensions={0} | all-to-all | bytes 1572864 | tf_op jit(solution)/shard_map/all_to_all | solution.py:203
  305.6 0.0 copy-done.3
  305.6 3.7 %convolution_bitcast_fusion.1 = f32[1,256,1024]{2,1,0:T(8,128)} fusion(f32[768,256]{1,0:T(8,128)S(1)} %bitcast.27, f32[768,1024]{1,0:T(8,128)S(1)} %copy-done.3), kind=kOutput, calls=%fused_computation.19 | convolution fusion | flops 2415919104 | bytes 4980736 | tf_op jit(solution)/shard_map/dot_general | solution.py:205
  309.3 0.0 copy-done.1
  (2 shorter events, 0.0 us)
Async XLA Ops:
  0.0 14.8 %copy-start = (bf16[2,256,1024]{2,1,0:T(8,128)(2,1)S(1)}, bf16[2,256,1024]{2,1,0:T(8,128)(2,1)}, u32[]{:S(2)}) copy-start(bf16[2,256,1024]{2,1,0:T(8,128)(2,1)} %param.8) | copy-start | bytes 3145732
  29.3 61.0 %all-to-all-start.2 = ((bf16[8,2,3,96,256]{4,3,2,1,0:T(8,128)(2,1)}), bf16[8,2,3,96,256]{4,3,2,1,0:T(8,128)(2,1)S(1)}, u32[]{:S(2)}, u32[]{:S(2)}) async-start(bf16[8,2,3,96,256]{4,3,2,1,0:T(8,128)(2,1)} %shard_map.75), calls=%async_computation.2 | async-start | bytes 4718592 | tf_op jit(solution)/shard_map/all_to_all | solution.py:193
  90.3 1.5 copy-start.4
  91.7 109.9 %all-to-all-start.1 = ((bf16[8,2,6,96,256]{4,3,2,1,0:T(8,128)(2,1)}), bf16[8,2,6,96,256]{4,3,2,1,0:T(8,128)(2,1)}, u32[]{:S(2)}, u32[]{:S(2)}) async-start(bf16[8,2,6,96,256]{4,3,2,1,0:T(8,128)(2,1)} %shard_map.74), calls=%async_computation.1 | async-start | bytes 9437184 | tf_op jit(solution)/shard_map/all_to_all | solution.py:193
  98.6 71.3 %collective-permute-start = (bf16[256,6144]{1,0:T(8,128)(2,1)S(1)}, bf16[256,6144]{1,0:T(8,128)(2,1)S(1)}, u32[]{:S(2)}, u32[]{:S(2)}) collective-permute-start(bf16[256,6144]{1,0:T(8,128)(2,1)S(1)} %slice.9), channel_id=1, source_target_pairs={{0,8},{8,16},{16,24},{1,9},{9,17},{17,25},{2,10},{10,18},{18,26},{... | collective-permute-start | bytes 9437192 | tf_op jit(solution)/shard_map/ppermute | solution.py:24
  169.9 1.6 copy-start.2
  201.6 58.2 %all-to-all-start = ((bf16[8,2,3,96,256]{4,3,2,1,0:T(8,128)(2,1)}), bf16[8,2,3,96,256]{4,3,2,1,0:T(8,128)(2,1)S(1)}, u32[]{:S(2)}, u32[]{:S(2)}) async-start(bf16[8,2,3,96,256]{4,3,2,1,0:T(8,128)(2,1)} %shard_map.73), calls=%async_computation | async-start | bytes 4718592 | tf_op jit(solution)/shard_map/all_to_all | solution.py:193
  256.1 22.0 %copy-start.6 = (s32[2048]{0:T(1024)S(1)}, s32[2048]{0:T(1024)}, u32[]{:S(2)}) copy-start(s32[2048]{0:T(1024)} %param.12) | copy-start | bytes 24580
  259.8 1.5 copy-start.5
  281.8 23.8 %copy-start.3 = (f32[768,1024]{1,0:T(8,128)S(1)}, f32[768,1024]{1,0:T(8,128)}, u32[]{:S(2)}) copy-start(f32[768,1024]{1,0:T(8,128)} %fusion.5) | copy-start | bytes 9437188
  281.9 27.4 %copy-start.1 = (bf16[2,256,1024]{2,1,0:T(8,128)(2,1)S(1)}, bf16[2,256,1024]{2,1,0:T(8,128)(2,1)}, u32[]{:S(2)}) copy-start(bf16[2,256,1024]{2,1,0:T(8,128)(2,1)} %param.8) | copy-start | bytes 3145732
where the time goes:
time: 310 us; the launch traced here: 309 us
  waiting for transfers between devices  123 us (40%)
  Pallas kernels  102 us (33%)
  matrix products  29.9 us (10%)
  blocking collectives  23.7 us (8%)
  starting transfers between devices  18.3 us (6%)
  local copies, waits for them, and re-layouts  8.6 us (3%)
  other arithmetic  3.17 us (1%)
    ppermute x1, waiting for transfers between devices, from_behind(): return lax.ppermute(block, axis, route)  67.5 us
    pallas_call x3, Pallas kernels, beams(): pl.pallas_call(beam_kernel, grid=(total // tile,), out_shape=jax.ShapeDty...  57 us
    all_to_all x3, waiting for transfers between devices, body(): got = lax.all_to_all(block, 'feed', split_axis=0, concat_axis=0, tiled=True)  55.8 us
    pallas_call x3, Pallas kernels, bank(): pl.pallas_call(functools.partial(bank_kernel, groups), grid=(count,), out...  45.2 us
    all_to_all x1, blocking collectives, body(): lax.all_to_all(ordered, 'feed', split_axis=0, concat_axis=0, tiled=True)  23.7 us
    all_to_all x3, starting transfers between devices, body(): got = lax.all_to_all(block, 'feed', split_axis=0, concat_axis=0, tiled=True)  14.5 us
    dot_general x1, matrix products, body(): table = jnp.einsum('sc,rcn->rsn', pick, jnp.asarray(make_table(FFT)))  11.9 us
    dot_general x1, matrix products, body(): jnp.dot(pick.astype(F32), delay_filter, precision=lax.Precision.HIGHEST)  8.45 us
  transfers between devices with their start and end apart: 4, of which 4 were waited for; matrix products, arithmetic and copies ran while one was open for 4% of the time, Pallas kernels for 24%

commit v1 on v0

--- a/solution.py
+++ b/solution.py
@@ -184,24 +184,38 @@
     rows = jnp.dot(pick.astype(F32), delay_filter, precision=lax.Precision.HIGHEST)
     order = (beam_order[None, :] == jnp.arange(total_beams, dtype=jnp.int32)[:, None]).astype(BF)
 
-    powers = jnp.zeros((slots, total_beams), F32)
-    outgoing = [
-        run_bank(earlier, voltages, window, table, gain, groups, first, count)
-        for first, count in PARTS
-    ]
-    for at, block in enumerate(outgoing):
-        got = lax.all_to_all(block, "feed", split_axis=0, concat_axis=0, tiled=True)
-        if at == len(outgoing) - 1:
-            powers, rows = lax.optimization_barrier((powers, rows))
-        powers = run_beams(got, beam_weights, powers)
-    powers = powers * (1.0 / frames_here)
-    high = powers.astype(BF)
-    low = (powers - high.astype(F32)).astype(BF)
-    ordered = jnp.dot(jnp.concatenate([high, low], axis=0), order, preferred_element_type=F32)
-    ordered = ordered[:slots] + ordered[slots:]
-    ordered = jnp.transpose(ordered.reshape(slots, groups, total_beams // groups), (1, 0, 2))
-    owned = lax.all_to_all(ordered, "feed", split_axis=0, concat_axis=0, tiled=True)
-    owned = owned.reshape(LIVE, total_beams // groups)
+    def exchange(block):
+        return lax.all_to_all(block, "feed", split_axis=0, concat_axis=0, tiled=True)
+
+    def by_owner(ordered):
+        return jnp.transpose(ordered.reshape(slots, groups, total_beams // groups), (1, 0, 2))
+
+    none = jnp.zeros((slots, total_beams), F32)
+    powers = none
+    for at, (first, count) in enumerate(PARTS):
+        if at == len(PARTS) - 1:
+            earlier, powers = lax.optimization_barrier((earlier, powers))
+        block = run_bank(earlier, voltages, window, table, gain, groups, first, count)
+        got = exchange(block)
+        if at == len(PARTS) - 1:
+            break
+        if at:
+            waiting = got
+        else:
+            powers = run_beams(got, beam_weights, powers)
+    powers = run_beams(waiting, beam_weights, powers)
+    powers, rows = lax.optimization_barrier((powers * (1.0 / frames_here), rows))
+    high = lax.reduce_precision(powers, 8, 7)
+    pair = jnp.concatenate([high.astype(BF), (powers - high).astype(BF)], axis=0)
+    ordered = jnp.dot(pair, order, preferred_element_type=F32)
+    ordered = by_owner(ordered[:slots] + ordered[slots:])
+    got, ordered = lax.optimization_barrier((got, ordered))
+    owned = exchange(ordered)
+    last = (run_beams(got, beam_weights, none) * (1.0 / frames_here)).astype(BF)
+    last = by_owner(jnp.dot(last, order, preferred_element_type=F32).astype(BF))
+    owned, last = lax.optimization_barrier((owned, last))
+    last = exchange(last)
+    owned = (owned + last.astype(F32)).reshape(LIVE, total_beams // groups)
     filtered = lax.dot_general(
         owned, rows, (((0,), (0,)), ((), ())), precision=lax.Precision.HIGHEST,
         preferred_element_type=F32,

time: 310 us -> 309 us (level)
  blocking collectives: 23.7 us -> 16.8 us
  matrix products: 29.9 us -> 36.4 us
  waiting for transfers between devices: 123 us -> 118 us
  starting transfers between devices: 18.3 us -> 22.1 us
    ppermute x1, waiting for transfers between devices: 67.5 us -> 51 us  [from_behind(): return lax.ppermute(block, axis, route)]
    all_to_all x3 -> x4, waiting for transfers between devices: 55.8 us -> 66.8 us  [exchange(): lax.all_to_all(block, 'feed', split_axis=0, concat_axis=0, tiled=True)]
    all_to_all x1, blocking collectives: 23.7 us -> 16.8 us  [exchange(): lax.all_to_all(block, 'feed', split_axis=0, concat_axis=0, tiled=True)]
    dot_general x1 -> x2, matrix products: 3.66 us -> 8.23 us  [the longest x1 4.57 us: body(): last = by_owner(jnp.dot(last, order, preferred_element_type=F32).astype(BF))]
    all_to_all x3 -> x4, starting transfers between devices: 14.5 us -> 18.3 us  [exchange(): lax.all_to_all(block, 'feed', split_axis=0, concat_axis=0, tiled=True)]
  transfers between devices with their start and end apart: 4 -> 5, of which waited for: 4 -> 5; matrix products, arithmetic and copies ran while one was open for 4% -> 7% of each run, Pallas kernels for 24% -> 29%
where the time goes in v1:
time: 309 us; the launch traced here: 308 us
  waiting for transfers between devices  118 us (38%)
  Pallas kernels  102 us (33%)
  matrix products  36.4 us (12%)
  starting transfers between devices  22.1 us (7%)
  blocking collectives  16.8 us (5%)
  local copies, waits for them, and re-layouts  9.46 us (3%)
  other arithmetic  3.32 us (1%)
    all_to_all x4, waiting for transfers between devices, exchange(): lax.all_to_all(block, 'feed', split_axis=0, concat_axis=0, tiled=True)  66.8 us
    pallas_call x3, Pallas kernels, beams(): pl.pallas_call(beam_kernel, grid=(total // tile,), out_shape=jax.ShapeDty...  57 us
    ppermute x1, waiting for transfers between devices, from_behind(): return lax.ppermute(block, axis, route)  51 us
    pallas_call x3, Pallas kernels, bank(): pl.pallas_call(functools.partial(bank_kernel, groups), grid=(count,), out...  45.2 us
    all_to_all x4, starting transfers between devices, exchange(): lax.all_to_all(block, 'feed', split_axis=0, concat_axis=0, tiled=True)  18.3 us
    all_to_all x1, blocking collectives, exchange(): lax.all_to_all(block, 'feed', split_axis=0, concat_axis=0, tiled=True)  16.8 us
    dot_general x1, matrix products, body(): table = jnp.einsum('sc,rcn->rsn', pick, jnp.asarray(make_table(FFT)))  11.9 us
    dot_general x1, matrix products, body(): jnp.dot(pick.astype(F32), delay_filter, precision=lax.Precision.HIGHEST)  8.45 us
  transfers between devices with their start and end apart: 5, of which 5 were waited for; matrix products, arithmetic and copies ran while one was open for 7% of the time, Pallas kernels for 29%

profile of v1, /device:TPU:0, one launch (start us, length us, event | category | flops | bytes accessed | tf_op | source)
XLA Modules:
  0.0 308.2 jit_solution(1474693813114243192)
XLA Ops:
  0.0 0.0 copy-start
  0.0 0.9 fusion.33.window_ref
  0.9 0.8 eq.76
  1.7 0.9 fusion.4
  2.6 0.3 fusion.5
  2.9 11.9 %convolution_bitcast_fusion.table_ref = bf16[2,768,2048]{2,1,0:T(8,128)(2,1)} fusion(bf16[2,1024,2048]{2,1,0:T(8,128)(2,1)} %constant.62.clone, s32[1024]{0:T(1024)S(1)} %convert_element_type.30, pred[1024]{0:T(1024)(128)(4,1)S(1)} %fusion.4), kind=kOutput, calls=%fused_computation.9 | convolution fusion | flops 6444023808 | bytes 14685184 | tf_op jit(solution)/shard_map/sc,rcn->rsn/dot_general | solution.py:182
  14.9 0.0 copy-done
  14.9 1.9 fusion.20.gain_ref
  16.8 12.6 %shard_map.73 = bf16[8,2,3,96,256]{4,3,2,1,0:T(8,128)(2,1)} custom-call(bf16[256,24576]{1,0:T(8,128)(2,1)} %frame_ref.5, bf16[256,24576]{1,0:T(8,128)(2,1)} %frame_ref.5, f32[4,2048]{1,0:T(4,128)} %fusion.33.window_ref, bf16[2,768,2048]{2,1,0:T(8,128)(2,1)} %convolution_bitcast_fusion.table_ref, bf16[2,768,256]{2,1,0:T(8,128)(2,1)} %fusion.20.gain_ref), custom_call_target="tpu_custom_call" | custom-call | flops 4831838208 | bytes 11796480 | tf_op jit(solution)/shard_map/pallas_call | solution.py:76
  29.3 6.3 %all-to-all-start = ((bf16[8,2,3,96,256]{4,3,2,1,0:T(8,128)(2,1)}), bf16[8,2,3,96,256]{4,3,2,1,0:T(8,128)(2,1)S(1)}, u32[]{:S(2)}, u32[]{:S(2)}) async-start(bf16[8,2,3,96,256]{4,3,2,1,0:T(8,128)(2,1)} %shard_map.73), calls=%async_computation | async-start | bytes 4718592 | tf_op jit(solution)/shard_map/all_to_all | solution.py:188
  35.6 20.1 %shard_map.76 = bf16[8,2,6,96,256]{4,3,2,1,0:T(8,128)(2,1)} custom-call(bf16[256,24576]{1,0:T(8,128)(2,1)} %frame_ref.5, bf16[256,24576]{1,0:T(8,128)(2,1)} %frame_ref.5, f32[4,2048]{1,0:T(4,128)} %fusion.33.window_ref, bf16[2,768,2048]{2,1,0:T(8,128)(2,1)} %convolution_bitcast_fusion.table_ref, bf16[2,768,256]{2,1,0:T(8,128)(2,1)} %fusion.20.gain_ref), custom_call_target="tpu_custom_call" | custom-call | flops 9663676416 | bytes 17301504 | tf_op jit(solution)/shard_map/pallas_call | solution.py:76
  55.7 34.6 %all-to-all-done.got_ref = bf16[8,2,3,96,256]{4,3,2,1,0:T(8,128)(2,1)S(1)} async-done(((bf16[8,2,3,96,256]{4,3,2,1,0:T(8,128)(2,1)}), bf16[8,2,3,96,256]{4,3,2,1,0:T(8,128)(2,1)S(1)}, u32[]{:S(2)}, u32[]{:S(2)}) %all-to-all-start) | async-done | bytes 2359328 | tf_op jit(solution)/shard_map/all_to_all | solution.py:188
  90.3 0.0 copy-start.4
  90.3 1.4 copy-done.4
  91.7 4.6 %all-to-all-start.2 = ((bf16[8,2,6,96,256]{4,3,2,1,0:T(8,128)(2,1)}), bf16[8,2,6,96,256]{4,3,2,1,0:T(8,128)(2,1)}, u32[]{:S(2)}, u32[]{:S(2)}) async-start(bf16[8,2,6,96,256]{4,3,2,1,0:T(8,128)(2,1)} %shard_map.76), calls=%async_computation.2 | async-start | bytes 9437184 | tf_op jit(solution)/shard_map/all_to_all | solution.py:188
  96.3 2.2 slice.9
  98.6 3.8 %collective-permute-start = (bf16[256,6144]{1,0:T(8,128)(2,1)S(1)}, bf16[256,6144]{1,0:T(8,128)(2,1)S(1)}, u32[]{:S(2)}, u32[]{:S(2)}) collective-permute-start(bf16[256,6144]{1,0:T(8,128)(2,1)S(1)} %slice.9), channel_id=1, source_target_pairs={{0,8},{8,16},{16,24},{1,9},{9,17},{17,25},{2,10},{10,18},{18,26},{... | collective-permute-start | bytes 9437192 | tf_op jit(solution)/shard_map/ppermute | solution.py:24
  102.4 1.0 broadcast_in_dim.9.before_ref
  103.3 15.5 %shard_map.74.before_ref = f32[96,2048]{1,0:T(8,128)} custom-call(bf16[8,2,3,96,256]{4,3,2,1,0:T(8,128)(2,1)} %copy-done.4, bf16[2,2048,2048]{2,1,0:T(8,128)(2,1)} %weight_ref.5, f32[96,2048]{1,0:T(8,128)} %broadcast_in_dim.9.before_ref), custom_call_target="tpu_custom_call" | custom-call | flops 9663676416 | bytes 19136512 | tf_op jit(solution)/shard_map/pallas_call | solution.py:120
  118.8 51.0 %collective-permute-done.hist_ref = bf16[256,6144]{1,0:T(8,128)(2,1)S(1)} collective-permute-done((bf16[256,6144]{1,0:T(8,128)(2,1)S(1)}, bf16[256,6144]{1,0:T(8,128)(2,1)S(1)}, u32[]{:S(2)}, u32[]{:S(2)}) %collective-permute-start) | collective-permute-done | bytes 3145760 | tf_op jit(solution)/shard_map/ppermute | solution.py:24
  169.8 0.0 copy-start.2
  169.8 1.6 copy-done.2
  171.5 12.5 %shard_map.75 = bf16[8,2,3,96,256]{4,3,2,1,0:T(8,128)(2,1)} custom-call(bf16[256,6144]{1,0:T(8,128)(2,1)} %copy-done.2, bf16[256,24576]{1,0:T(8,128)(2,1)} %frame_ref.5, f32[4,2048]{1,0:T(4,128)} %fusion.33.window_ref, bf16[2,768,2048]{2,1,0:T(8,128)(2,1)} %convolution_bitcast_fusion.table_ref, bf16[2,768,256]{2,1,0:T(8,128)(2,1)} %fusion.20.gain_ref), custom_call_target="tpu_custom_call" | custom-call | flops 4831838208 | bytes 11796480 | tf_op jit(solution)/shard_map/pallas_call | solution.py:76
  184.0 17.6 %all-to-all-done.2.got_ref = bf16[8,2,6,96,256]{4,3,2,1,0:T(8,128)(2,1)} async-done(((bf16[8,2,6,96,256]{4,3,2,1,0:T(8,128)(2,1)}), bf16[8,2,6,96,256]{4,3,2,1,0:T(8,128)(2,1)}, u32[]{:S(2)}, u32[]{:S(2)}) %all-to-all-start.2) | async-done | bytes 4718624 | tf_op jit(solution)/shard_map/all_to_all | solution.py:188
  201.6 3.6 %all-to-all-start.1 = ((bf16[8,2,3,96,256]{4,3,2,1,0:T(8,128)(2,1)}), bf16[8,2,3,96,256]{4,3,2,1,0:T(8,128)(2,1)S(1)}, u32[]{:S(2)}, u32[]{:S(2)}) async-start(bf16[8,2,3,96,256]{4,3,2,1,0:T(8,128)(2,1)} %shard_map.75), calls=%async_computation.1 | async-start | bytes 4718592 | tf_op jit(solution)/shard_map/all_to_all | solution.py:188
  205.2 8.4 %fusion.7 = f32[768,1024]{1,0:T(8,128)} fusion(f32[1024,1024]{1,0:T(8,128)} %param.10, s32[1024]{0:T(1024)S(1)} %convert_element_type.30, pred[1024]{0:T(1024)(128)(4,1)S(1)} %fusion.4), kind=kOutput, calls=%fused_computation.12 | convolution fusion | flops 9665249280 | bytes 7345152 | tf_op jit(solution)/shard_map/dot_general | solution.py:184
  213.7 0.0 copy-start.5
  213.7 25.9 %shard_map.77 = f32[96,2048]{1,0:T(8,128)} custom-call(bf16[8,2,6,96,256]{4,3,2,1,0:T(8,128)(2,1)} %all-to-all-done.2.got_ref, bf16[2,2048,2048]{2,1,0:T(8,128)(2,1)} %weight_ref.5, f32[96,2048]{1,0:T(8,128)} %shard_map.74.before_ref), custom_call_target="tpu_custom_call" | custom-call | flops 19327352832 | bytes 21495808 | tf_op jit(solution)/shard_map/pallas_call | solution.py:120
  239.6 1.2 broadcast_multiply_fusion
  240.8 0.1 reduce-precision_convert_fusion
  240.9 0.0 copy-done.5
  241.0 3.7 %fusion.1 = f32[192,2048]{1,0:T(8,128)S(1)} fusion(s32[2048]{0:T(1024)S(1)} %copy-done.5, bf16[96,2048]{1,0:T(8,128)(2,1)S(1)} %get-tuple-element.22, bf16[96,2048]{1,0:T(8,128)(2,1)S(1)} %get-tuple-element.21), kind=kOutput, calls=%fused_computation.2 | convolution fusion | flops 1616379904 | bytes 2367488 | tf_op jit(solution)/shard_map/dot_general | solution.py:210
  244.6 0.1 slice_add_fusion
  244.7 1.0 copy.16
  245.7 14.2 %all-to-all-done.1.got_ref = bf16[8,2,3,96,256]{4,3,2,1,0:T(8,128)(2,1)S(1)} async-done(((bf16[8,2,3,96,256]{4,3,2,1,0:T(8,128)(2,1)}), bf16[8,2,3,96,256]{4,3,2,1,0:T(8,128)(2,1)S(1)}, u32[]{:S(2)}, u32[]{:S(2)}) %all-to-all-start.1) | async-done | bytes 2359328 | tf_op jit(solution)/shard_map/all_to_all | solution.py:188
  259.8 0.0 copy-start.3
  259.8 1.5 copy-done.3
  261.3 3.8 %all-to-all-start.3 = ((f32[8,96,256]{2,1,0:T(8,128)}), f32[8,96,256]{2,1,0:T(8,128)S(1)}, u32[]{:S(2)}, u32[]{:S(2)}) async-start(f32[8,96,256]{2,1,0:T(8,128)} %bitcast.31), calls=%async_computation.3 | async-start | bytes 1572864 | tf_op jit(solution)/shard_map/all_to_all | solution.py:188
  265.1 15.6 %shard_map.78 = f32[96,2048]{1,0:T(8,128)} custom-call(bf16[8,2,3,96,256]{4,3,2,1,0:T(8,128)(2,1)} %copy-done.3, bf16[2,2048,2048]{2,1,0:T(8,128)(2,1)} %weight_ref.5, f32[96,2048]{1,0:T(8,128)} %broadcast_in_dim.9.before_ref), custom_call_target="tpu_custom_call" | custom-call | flops 9663676416 | bytes 19136512 | tf_op jit(solution)/shard_map/pallas_call | solution.py:120
  280.6 4.6 %fusion.13 = bf16[96,2048]{1,0:T(8,128)(2,1)S(1)} fusion(s32[2048]{0:T(1024)S(1)} %copy-done.5, f32[96,2048]{1,0:T(8,128)} %shard_map.78), kind=kOutput, calls=%fused_computation.15 | convolution fusion | flops 810090496 | bytes 1187840 | tf_op jit(solution)/shard_map/dot_general | solution.py:215
  285.2 0.0 copy-start.1
  285.3 0.5 all-to-all-done.3
  285.7 16.8 %all_to_all.25 = bf16[8,96,256]{2,1,0:T(8,128)(2,1)S(1)} all-to-all(bf16[8,96,256]{2,1,0:T(8,128)(2,1)S(1)} %bitcast.36), channel_id=1, replica_groups=mesh['tm'=4,'feed'=8] {'feed'}, dimensions={0} | all-to-all | bytes 786432 | tf_op jit(solution)/shard_map/all_to_all | solution.py:188
  302.5 0.1 convert_add_fusion
  302.6 5.6 %convolution_bitcast_fusion.1 = f32[1,256,1024]{2,1,0:T(8,128)} fusion(f32[768,256]{1,0:T(8,128)S(1)} %bitcast.34, f32[768,1024]{1,0:T(8,128)} %fusion.7), kind=kOutput, calls=%fused_computation.22 | convolution fusion | flops 2415919104 | bytes 4980736 | tf_op jit(solution)/shard_map/dot_general | solution.py:219
  308.2 0.0 copy-done.1
  (3 shorter events, 0.0 us)
Async XLA Ops:
  0.0 14.9 %copy-start = (bf16[2,256,1024]{2,1,0:T(8,128)(2,1)S(1)}, bf16[2,256,1024]{2,1,0:T(8,128)(2,1)}, u32[]{:S(2)}) copy-start(bf16[2,256,1024]{2,1,0:T(8,128)(2,1)} %param.8) | copy-start | bytes 3145732
  29.3 61.0 %all-to-all-start = ((bf16[8,2,3,96,256]{4,3,2,1,0:T(8,128)(2,1)}), bf16[8,2,3,96,256]{4,3,2,1,0:T(8,128)(2,1)S(1)}, u32[]{:S(2)}, u32[]{:S(2)}) async-start(bf16[8,2,3,96,256]{4,3,2,1,0:T(8,128)(2,1)} %shard_map.73), calls=%async_computation | async-start | bytes 4718592 | tf_op jit(solution)/shard_map/all_to_all | solution.py:188
  90.3 1.4 copy-start.4
  91.7 109.9 %all-to-all-start.2 = ((bf16[8,2,6,96,256]{4,3,2,1,0:T(8,128)(2,1)}), bf16[8,2,6,96,256]{4,3,2,1,0:T(8,128)(2,1)}, u32[]{:S(2)}, u32[]{:S(2)}) async-start(bf16[8,2,6,96,256]{4,3,2,1,0:T(8,128)(2,1)} %shard_map.76), calls=%async_computation.2 | async-start | bytes 9437184 | tf_op jit(solution)/shard_map/all_to_all | solution.py:188
  98.6 71.3 %collective-permute-start = (bf16[256,6144]{1,0:T(8,128)(2,1)S(1)}, bf16[256,6144]{1,0:T(8,128)(2,1)S(1)}, u32[]{:S(2)}, u32[]{:S(2)}) collective-permute-start(bf16[256,6144]{1,0:T(8,128)(2,1)S(1)} %slice.9), channel_id=1, source_target_pairs={{0,8},{8,16},{16,24},{1,9},{9,17},{17,25},{2,10},{10,18},{18,26},{... | collective-permute-start | bytes 9437192 | tf_op jit(solution)/shard_map/ppermute | solution.py:24
  169.8 1.6 copy-start.2
  201.6 58.2 %all-to-all-start.1 = ((bf16[8,2,3,96,256]{4,3,2,1,0:T(8,128)(2,1)}), bf16[8,2,3,96,256]{4,3,2,1,0:T(8,128)(2,1)S(1)}, u32[]{:S(2)}, u32[]{:S(2)}) async-start(bf16[8,2,3,96,256]{4,3,2,1,0:T(8,128)(2,1)} %shard_map.75), calls=%async_computation.1 | async-start | bytes 4718592 | tf_op jit(solution)/shard_map/all_to_all | solution.py:188
  213.7 27.3 %copy-start.5 = (s32[2048]{0:T(1024)S(1)}, s32[2048]{0:T(1024)}, u32[]{:S(2)}) copy-start(s32[2048]{0:T(1024)} %param.12) | copy-start | bytes 24580
  259.8 1.5 copy-start.3
  261.3 24.5 %all-to-all-start.3 = ((f32[8,96,256]{2,1,0:T(8,128)}), f32[8,96,256]{2,1,0:T(8,128)S(1)}, u32[]{:S(2)}, u32[]{:S(2)}) async-start(f32[8,96,256]{2,1,0:T(8,128)} %bitcast.31), calls=%async_computation.3 | async-start | bytes 1572864 | tf_op jit(solution)/shard_map/all_to_all | solution.py:188
  285.2 23.0 %copy-start.1 = (bf16[2,256,1024]{2,1,0:T(8,128)(2,1)S(1)}, bf16[2,256,1024]{2,1,0:T(8,128)(2,1)}, u32[]{:S(2)}) copy-start(bf16[2,256,1024]{2,1,0:T(8,128)(2,1)} %param.8) | copy-start | bytes 3145732
